TPU v7x, 128 devices: a whole 4x4x4 slice. The times are simulated.
128 devices in a mesh: grp: 4 (over y), lane: 32 (over x, z, core).
Axes of the slice: x: 4, y: 4, z: 4, core: 2. Of those that a mesh axis runs over, the one named last changes fastest.
Arguments:
- activations: bfloat16 [131072, 8192], P(('grp', 'lane')), may hold values from -60 to 60
- sketch: bfloat16 [8192, 256], replicated, may hold values from -0.0625 to 0.0625
Outputs:
- projection: float32 [8192, 256], P('lane')
All inputs are finite; a program needn't handle non-finite values.
Results may differ from a plain program's by a relative error of at most 0.00068.
Values sent between devices are 32-bit elements; how exact they have to be, the bound alone decides.
A program may use at most 128 MiB of HBM per device.

v0:
```python
import jax
import jax.numpy as jnp
from jax import lax
from jax.sharding import PartitionSpec as P


def local(activations, sketch):
    sampled = jnp.dot(activations, sketch, preferred_element_type=jnp.float32)
    sampled_half = sampled.astype(jnp.bfloat16)
    gram = jnp.dot(sampled.T, sampled, precision=lax.Precision.HIGHEST)
    width = activations.shape[1]
    share = width // lax.axis_size("lane")
    term = lax.dot_general(
        activations, sampled_half, (((0,), (0,)), ((), ())), preferred_element_type=jnp.float32
    )
    summed = lax.psum(term, ("grp", "lane"))
    cross = lax.dynamic_slice_in_dim(summed, lax.axis_index("lane") * share, share, 0)
    lower = jnp.linalg.cholesky(lax.psum(gram, ("grp", "lane")))
    return lax.linalg.triangular_solve(lower, cross, left_side=False, lower=True, transpose_a=True)


def solution(mesh):
    return jax.shard_map(
        local,
        mesh=mesh,
        in_specs=(P(("grp", "lane"), None), P()),
        out_specs=P("lane", None),
        check_vma=False,
    )
```

profile of v0, /device:TPU:0, one launch (start us, length us, event | category | flops | bytes accessed | tf_op | source)
XLA Modules:
  0.0 264.6 jit_solution(8640133929699016510)
XLA Ops:
  6.5 0.0 all-reduce.4.cloned.1.call-start
  6.5 0.0 copy-start
  6.5 9.9 %fusion.11 = f32[1024,256]{1,0:T(8,128)S(1)} fusion(bf16[1024,8192]{1,0:T(8,128)(2,1)} %param.2, bf16[8192,256]{1,0:T(8,128)(2,1)} %param.3), kind=kOutput, calls=%fused_computation.32 | convolution fusion | flops 4294967296 | bytes 22020096 | tf_op jit(solution)/shard_map/dot_general | solution.py:8
  16.4 1.9 copy-done
  18.3 6.7 %convolution_bitcast_fusion = f32[8192,256]{0,1:T(8,128)} fusion(bf16[1024,8192]{1,0:T(8,128)(2,1)S(1)} %copy-done, f32[1024,256]{1,0:T(8,128)S(1)} %fusion.11), kind=kOutput, calls=%fused_computation.2 | convolution fusion | flops 4295229440 | bytes 26214400 | tf_op jit(solution)/shard_map/dot_general | solution.py:13
  25.0 2.5 fusion.12
  27.5 0.0 all-reduce.4.cloned.1.call-update
  27.6 165.0 %all-reduce.4.cloned.1.call-done = (f32[8192,256]{0,1:T(8,128)}, f32[256,256]{0,1:T(8,128)}) async-done(((f32[8192,256]{0,1:T(8,128)}, f32[256,256]{0,1:T(8,128)}), (f32[8192,256]{0,1:T(8,128)}, f32[256,256]{0,1:T(8,128)})) %all-reduce.4.cloned.1.call-update) | async-done | bytes 8650768 | tf_op jit(solution)/shard_map/psum | solution.py:16
  192.6 1.1 copy.4
  193.7 1.0 fusion.1
  194.7 11.7 %cholesky.50 = f32[128,128]{1,0:T(8,128)S(1)} custom-call(f32[128,128]{1,0:T(8,128)S(1)} %cholesky.118), custom_call_target="Cholesky" | custom-call | tf_op jit(solution)/shard_map/jit(cholesky)/cholesky | solution.py:18
  206.4 9.8 %custom-call.14 = f32[1,128,128]{1,2,0:T(8,128)S(1)} custom-call(f32[1,128,128]{2,1,0:T(8,128)S(1)} %get-tuple-element.28), custom_call_target="InvertDiagBlocksLowerTriangular" | custom-call | tf_op jit(solution)/shard_map/jit(cholesky)/cholesky | solution.py:18
  216.3 0.2 constant_dynamic-update-slice_fusion.1
  216.5 0.3 convolution_subtract_fusion.1
  216.8 11.7 %cholesky.105 = f32[128,128]{1,0:T(8,128)S(1)} custom-call(f32[128,128]{1,0:T(8,128)S(1)} %convolution_subtract_fusion.1), custom_call_target="Cholesky" | custom-call | tf_op jit(solution)/shard_map/jit(cholesky)/cholesky | solution.py:18
  228.5 0.8 compare_reduce_fusion
  230.6 0.1 triangular_solve.58
  230.7 3.8 %while.1 = (s32[]{:T(128)}, f32[256,256]{1,0:T(8,128)S(1)}, s32[2,2]{1,0:T(2,128)S(1)}, f32[2,128,128]{2,1,0:T(8,128)S(1)}, s32[]{:T(128)}) while((s32[]{:T(128)}, f32[256,256]{1,0:T(8,128)S(1)}, s32[2,2]{1,0:T(2,128)S(1)}, f32[2,128,128]{2,1,0:T(8,128)S(1)}, s32[]{:T(128)}) %tuple.23), condition=%wide.while_cond, body=%wide.while_body.sunk | while | flops 2 | bytes 131181 | solution.py:19
  230.7 0.6 fusion.23
  231.3 1.3 bitcast_dynamic-update-slice_fusion.2
  232.6 0.6 fusion.23
  233.2 1.3 bitcast_dynamic-update-slice_fusion.2
  234.5 19.7 %custom-call.15 = f32[2,128,128]{1,2,0:T(8,128)S(1)} custom-call(f32[2,128,128]{2,1,0:T(8,128)S(1)} %get-tuple-element.12), custom_call_target="InvertDiagBlocksLowerTriangular" | custom-call | tf_op jit(solution)/shard_map/triangular_solve | solution.py:19
  254.2 1.2 fusion.2
  255.4 1.2 convolution_subtract_fusion
  256.6 0.3 fusion.4
  257.0 0.8 copy.5
  (10 shorter events, 0.2 us)
Async XLA Ops:
  6.5 186.1 %all-reduce.4.cloned.1.call-start = ((), (), s32[]{:S(2)}) async-start(), calls=%async_computation | async-start | bytes 17301504 | tf_op jit(solution)/shard_map/psum | solution.py:16
  6.5 11.7 %copy-start = (bf16[1024,8192]{1,0:T(8,128)(2,1)S(1)}, bf16[1024,8192]{1,0:T(8,128)(2,1)}, u32[]{:S(2)}) copy-start(bf16[1024,8192]{1,0:T(8,128)(2,1)} %param.2) | copy-start | bytes 50331652
Sparse Core Ops, SparseCore 0:
  27.6 164.9 all-reduce.3
where the time goes:
time: 265 us
  waiting for transfers between devices  165 us (62%)
  other arithmetic  54.8 us (21%)
  matrix products  22.3 us (8%)
  between operations  14.7 us (6%)
  local copies, waits for them, and re-layouts  7.66 us (3%)
    psum x1, waiting for transfers between devices, local(): summed = lax.psum(term, ('grp', 'lane'))  165 us
    another operation x6, other arithmetic, local(): lower = jnp.linalg.cholesky(lax.psum(gram, ('grp', 'lane')))  34.1 us
    another operation x4, other arithmetic, local(): lax.linalg.triangular_solve(lower, cross, left_side=False, lower=True, tr...  19.7 us
    dot_general x1, matrix products, local(): sampled = jnp.dot(activations, sketch, preferred_element_type=jnp.float32)  9.87 us
    dot_general x1, matrix products, local(): lax.dot_general(activations, sampled_half, (((0,), (0,)), ((), ())), pref...  6.71 us
  transfers between devices with their start and end apart: 1, of which 1 were waited for; matrix products, arithmetic and copies ran while one was open for 0% of the time, Pallas kernels for 0%

commit v1 on v0

v1 whole, which is shorter than its diff:
```python
import functools

import jax
import jax.numpy as jnp
from jax import lax
from jax.experimental import pallas as pl
from jax.experimental.pallas import tpu as pltpu
from jax.sharding import PartitionSpec as P

MESH = pl.DeviceIdType.MESH
F32, BF16 = jnp.float32, jnp.bfloat16
NK, KW = 8, 1024
RX, RZ, RY = 80, 80, 96
Y0, HXZ, HY, HY1 = RX + RZ, (RX + RZ) // 2, RY // 2, RY // 4


def mod4(v):
    return lax.rem(v, 4)


def wait(ref, sem):
    pltpu.make_async_copy(ref, ref, sem).wait()


def kernel(
    a_hbm, s_hbm, c_out, g_out,
    a, s, acc, ht, g, gh, gr, gy, gf, q, r, p, cb,
    rx, rz, ry, rx2, rz2, ry1, ry2, rq3, ry13, ry23,
    asem, ssem, gsem, qsem, rsem, ss1, rs1, ss2, rs2, ss3, rs3, ss4, rs4,
):
    y, lane = lax.axis_index("grp"), lax.axis_index("lane")
    x, z, c = lax.div(lane, 8), mod4(lax.div(lane, 2)), lax.rem(lane, 2)

    def dev(x_, y_, z_, c_):
        return {"grp": y_, "lane": (x_ * 4 + z_) * 2 + c_}

    def send(src, dst, ss, rs, to):
        pltpu.make_async_remote_copy(
            src_ref=src, dst_ref=dst, send_sem=ss, recv_sem=rs, device_id=to, device_id_type=MESH
        ).start()

    def load(i):
        cols = pl.ds(i * KW, KW)
        return (
            pltpu.make_async_copy(s_hbm.at[cols, :], s.at[cols, :], ssem.at[i]),
            pltpu.make_async_copy(a_hbm.at[:, cols], a.at[:, cols], asem.at[i]),
        )

    for i in range(NK):
        for copy in load(i):
            copy.start()

    barrier = pltpu.get_barrier_semaphore()
    pl.semaphore_signal(barrier, inc=1, device_id=dev(x, y, z, 1 - c), device_id_type=MESH)

    def greet(d, carry):
        to = dev(mod4(x + lax.div(d, 4)), y, mod4(z + lax.rem(d, 4)), c)
        pl.semaphore_signal(barrier, inc=1, device_id=to, device_id_type=MESH)
        return carry

    lax.fori_loop(1, 16, greet, 0)
    for d in range(1, 4):
        pl.semaphore_signal(barrier, inc=1, device_id=dev(x, mod4(y + d), z, c), device_id_type=MESH)

    acc[...] = jnp.zeros_like(acc)

    def sample(i, carry):
        cols = pl.ds(pl.multiple_of(i * KW, KW), KW)
        for copy in load_dyn(cols, i):
            copy.wait()
        acc[...] += jnp.dot(a[:, cols], s[cols, :], preferred_element_type=F32)
        return carry

    def load_dyn(cols, i):
        return (
            pltpu.make_async_copy(s_hbm.at[cols, :], s.at[cols, :], ssem.at[i]),
            pltpu.make_async_copy(a_hbm.at[:, cols], a.at[:, cols], asem.at[i]),
        )

    lax.fori_loop(0, NK, sample, 0)

    def mm(u, v):
        return jnp.dot(u, v, preferred_element_type=F32)

    def split(i, carry):
        g0, m = carry
        rows = pl.ds(pl.multiple_of(i * 256, 256), 256)
        v = acc[rows, :]
        hi = v.astype(BF16)
        rest = v - hi.astype(F32)
        mid = rest.astype(BF16)
        lo = (rest - mid.astype(F32)).astype(BF16)
        hit = hi.astype(F32).T.astype(BF16)
        ht[:, rows] = hit
        g0 = g0 + mm(hit, hi) + mm(mid.astype(F32).T.astype(BF16), mid)
        return g0, m + mm(hit, mid) + mm(hit, lo)

    zero = jnp.zeros((256, 256), F32)
    g0, m = lax.fori_loop(0, 4, split, (zero, zero))
    g[...] = g0 + m + m.T

    pl.semaphore_wait(barrier, 19)
    other = pl.ds(pl.multiple_of((1 - c) * 128, 128), 128)
    mine = pl.ds(pl.multiple_of(c * 128, 128), 128)
    core = dev(x, y, z, 1 - c)
    send(g.at[other, :], gh, gsem.at[0], gsem.at[1], core)

    def order(t):
        dx, dz = mod4(t + 1), mod4(lax.div(t, 4) + t + 1)
        return dx, dz, mod4(x + dx), mod4(z + dz)

    def block(x_, z_, c_):
        lb = (x_ * 4 + z_) * 2 + c_
        return mm(ht[...], a[:, pl.ds(pl.multiple_of(lb * 256, 256), 256)])

    def give(t, carry):
        _, _, x_, z_ = order(t)
        b = block(x_, z_, 1 - c)
        q[x_, z_, 0] = b[:, :128]
        q[x_, z_, 1] = b[:, 128:]
        send(q.at[x_, z_], r.at[x_, z_], qsem.at[x_ * 4 + z_], rsem.at[x_ * 4 + z_], core)
        return carry

    lax.fori_loop(0, 16, give, 0)

    wait(gh, gsem.at[1])
    g[mine, :] += gh[...]

    def piece(x_, z_):
        return pl.ds(pl.multiple_of(c * 128 + (x_ * 4 + z_) * 8, 8), 8)

    def scatter_gram(d, carry):
        x_, z_ = mod4(x + lax.div(d, 4)), mod4(z + lax.rem(d, 4))
        send(g.at[piece(x_, z_), :], gr.at[d - 1], gsem.at[2], gsem.at[3], dev(x_, y, z_, c))
        return carry

    lax.fori_loop(1, 16, scatter_gram, 0)

    def own(t, carry):
        dx, dz, x_, z_ = order(t)
        b = block(x_, z_, c)
        wait(r.at[x_, z_], rsem.at[x_ * 4 + z_])
        p[x_, z_, 0] = b[:, :128] + r[x_, z_, 0]
        p[x_, z_, 1] = b[:, 128:] + r[x_, z_, 1]

        @pl.when(dx != 0)
        def _():
            send(p.at[x_, z_, :, pl.ds(0, RX), :], rx.at[dx - 1, z_], ss1.at[dx - 1], rs1.at[dx - 1], dev(x_, y, z, c))

        @pl.when(dz != 0)
        def _():
            send(p.at[x_, z_, :, pl.ds(RX, RZ), :], rz.at[dz - 1, x_], ss1.at[dz + 2], rs1.at[dz + 2], dev(x, y, z_, c))

        for d in range(1, 4):
            y_ = mod4(y + d)
            rows = pl.ds(pl.multiple_of(Y0 + lax.div(y_, 2) * HY, 8), HY)
            send(p.at[x_, z_, lax.rem(y_, 2), rows, :], ry.at[d - 1, x_, z_], ss1.at[5 + d], rs1.at[5 + d], dev(x, y_, z, c))
        return carry

    lax.fori_loop(0, 16, own, 0)

    wait(gr, gsem.at[3])
    gy[y] = g[piece(x, z), :] + jnp.sum(gr[...], axis=0)
    for d in range(1, 4):
        send(gy.at[y], gy.at[y], gsem.at[4], gsem.at[5], dev(x, mod4(y + d), z, c))
    wait(gy.at[pl.ds(0, 3)], gsem.at[5])
    gf[piece(x, z), :] = (gy[0] + gy[1]) + (gy[2] + gy[3])

    def gather_gram(d, carry):
        x_, z_ = mod4(x + lax.div(d, 4)), mod4(z + lax.rem(d, 4))
        send(gf.at[piece(x, z), :], gf.at[piece(x, z), :], gsem.at[6], gsem.at[7], dev(x_, y, z_, c))
        return carry

    lax.fori_loop(1, 16, gather_gram, 0)

    ch = lax.rem(y, 2)
    y0 = Y0 + lax.div(y, 2) * HY
    rows_y = pl.ds(pl.multiple_of(y0, 8), HY)
    rows_1 = pl.ds(pl.multiple_of(y0, 8), HY1)
    rows_2 = pl.ds(pl.multiple_of(y0 + HY1, 8), HY - HY1)
    rows_x, rows_z = pl.ds(0, RX), pl.ds(RX, RZ)
    for d in range(3):
        wait(rx.at[d], rs1.at[d])
    for k in range(4):
        p[x, k, :, rows_x, :] += rx[0, k] + rx[1, k] + rx[2, k]
    for d in range(1, 4):
        z_ = mod4(z + d)
        send(p.at[x, z_, :, rows_x, :], rx2.at[d - 1], ss2.at[d - 1], rs2.at[d - 1], dev(x, y, z_, c))
    for d in range(3):
        wait(rz.at[d], rs1.at[3 + d])
    for k in range(4):
        p[k, z, :, rows_z, :] += rz[0, k] + rz[1, k] + rz[2, k]
    for d in range(1, 4):
        x_ = mod4(x + d)
        send(p.at[x_, z, :, rows_z, :], rz2.at[d - 1], ss2.at[2 + d], rs2.at[2 + d], dev(x_, y, z, c))
    for d in range(3):
        wait(ry.at[d], rs1.at[6 + d])
    for k in range(4):
        p[k, :, ch, rows_y, :] += ry[0, k] + ry[1, k] + ry[2, k]
    for d in range(1, 4):
        x_, z_ = mod4(x + d), mod4(z + d)
        send(p.at[x_, :, ch, rows_1, :], ry1.at[d - 1], ss2.at[5 + d], rs2.at[5 + d], dev(x_, y, z, c))
        send(p.at[:, z_, ch, rows_2, :], ry2.at[d - 1], ss2.at[8 + d], rs2.at[8 + d], dev(x, y, z_, c))

    wait(gf.at[pl.ds(0, 120), :], gsem.at[7])
    send(gf.at[mine, :], gf.at[mine, :], gsem.at[8], gsem.at[9], core)

    for d in range(3):
        wait(rx2.at[d], rs2.at[d])
    p[x, z, :, rows_x, :] += rx2[0] + rx2[1] + rx2[2]
    for d in range(3):
        wait(rz2.at[d], rs2.at[3 + d])
    p[x, z, :, rows_z, :] += rz2[0] + rz2[1] + rz2[2]
    for d in range(1, 4):
        y_ = mod4(y + d)
        rows = pl.ds(pl.multiple_of(lax.div(y_, 2) * HXZ, 8), HXZ)
        send(p.at[x, z, lax.rem(y_, 2), rows, :], rq3.at[d - 1], ss3.at[d - 1], rs3.at[d - 1], dev(x, y_, z, c))
    for d in range(3):
        wait(ry1.at[d], rs2.at[6 + d])
    p[x, :, ch, rows_1, :] += ry1[0] + ry1[1] + ry1[2]
    for d in range(1, 4):
        z_ = mod4(z + d)
        send(p.at[x, z_, ch, rows_1, :], ry13.at[d - 1], ss3.at[2 + d], rs3.at[2 + d], dev(x, y, z_, c))
    for d in range(3):
        wait(ry2.at[d], rs2.at[9 + d])
    p[:, z, ch, rows_2, :] += ry2[0] + ry2[1] + ry2[2]
    for d in range(1, 4):
        x_ = mod4(x + d)
        send(p.at[x_, z, ch, rows_2, :], ry23.at[d - 1], ss3.at[5 + d], rs3.at[5 + d], dev(x_, y, z, c))

    rows_q = pl.ds(pl.multiple_of(lax.div(y, 2) * HXZ, 8), HXZ)
    for d in range(3):
        wait(rq3.at[d], rs3.at[d])
    cb[ch, rows_q, :] = p[x, z, ch, rows_q, :] + (rq3[0] + rq3[1] + rq3[2])
    for d in range(1, 4):
        send(cb.at[ch, rows_q, :], cb.at[ch, rows_q, :], ss4.at[d - 1], rs4.at[d - 1], dev(x, mod4(y + d), z, c))
    for d in range(3):
        wait(ry13.at[d], rs3.at[3 + d])
        wait(ry23.at[d], rs3.at[6 + d])
    cb[ch, rows_1, :] = p[x, z, ch, rows_1, :] + (ry13[0] + ry13[1] + ry13[2])
    cb[ch, rows_2, :] = p[x, z, ch, rows_2, :] + (ry23[0] + ry23[1] + ry23[2])
    for d in range(1, 4):
        send(cb.at[ch, rows_y, :], cb.at[ch, rows_y, :], ss4.at[d + 2], rs4.at[d + 2], dev(x, mod4(y + d), z, c))

    def sent(t, carry):
        x_, z_ = lax.div(t, 4), lax.rem(t, 4)
        wait(q.at[x_, z_], qsem.at[t])
        return carry

    lax.fori_loop(0, 16, sent, 0)
    wait(gh, gsem.at[0])
    wait(gr, gsem.at[2])
    wait(gy.at[pl.ds(0, 3)], gsem.at[4])
    wait(gf.at[pl.ds(0, 120), :], gsem.at[6])
    wait(gf.at[mine, :], gsem.at[8])
    for d in range(3):
        wait(rx.at[d], ss1.at[d])
        wait(rz.at[d], ss1.at[3 + d])
        wait(ry.at[d], ss1.at[6 + d])
        wait(rx2.at[d], ss2.at[d])
        wait(rz2.at[d], ss2.at[3 + d])
        wait(ry1.at[d], ss2.at[6 + d])
        wait(ry2.at[d], ss2.at[9 + d])
        wait(rq3.at[d], ss3.at[d])
        wait(ry13.at[d], ss3.at[3 + d])
        wait(ry23.at[d], ss3.at[6 + d])
        wait(rq3.at[d], ss4.at[d])
        wait(cb.at[ch, rows_y, :], ss4.at[3 + d])
    wait(gf.at[other, :], gsem.at[9])
    g_out[...] = gf[...]
    for d in range(3):
        wait(rq3.at[d], rs4.at[d])
        wait(cb.at[ch, rows_y, :], rs4.at[3 + d])
    c_out[...] = cb[...]


def local(activations, sketch):
    dma = pltpu.SemaphoreType.DMA
    vmem = pltpu.VMEM
    crossed, gram = pl.pallas_call(
        kernel,
        out_shape=(jax.ShapeDtypeStruct((2, 256, 128), F32), jax.ShapeDtypeStruct((256, 256), F32)),
        in_specs=[pl.BlockSpec(memory_space=pl.ANY)] * 2,
        out_specs=[pl.BlockSpec(memory_space=pltpu.VMEM)] * 2,
        scratch_shapes=[
            vmem((1024, 8192), BF16), vmem((8192, 256), BF16), vmem((1024, 256), F32), vmem((256, 1024), BF16),
            vmem((256, 256), F32), vmem((128, 256), F32), vmem((15, 8, 256), F32), vmem((4, 8, 256), F32), vmem((256, 256), F32),
            vmem((4, 4, 2, 256, 128), F32), vmem((4, 4, 2, 256, 128), F32), vmem((4, 4, 2, 256, 128), F32), vmem((2, 256, 128), F32),
            vmem((3, 4, 2, RX, 128), F32), vmem((3, 4, 2, RZ, 128), F32), vmem((3, 4, 4, HY, 128), F32),
            vmem((3, 2, RX, 128), F32), vmem((3, 2, RZ, 128), F32), vmem((3, 4, HY1, 128), F32), vmem((3, 4, HY - HY1, 128), F32),
            vmem((3, HXZ, 128), F32), vmem((3, HY1, 128), F32), vmem((3, HY - HY1, 128), F32),
            dma((NK,)), dma((NK,)), dma((10,)), dma((16,)), dma((16,)),
            dma((9,)), dma((9,)), dma((12,)), dma((12,)), dma((9,)), dma((9,)), dma((6,)), dma((6,)),
        ],
        compiler_params=pltpu.CompilerParams(collective_id=0, has_side_effects=True, vmem_limit_bytes=56 << 20),
        cost_estimate=pl.CostEstimate(flops=9_000_000_000, bytes_accessed=22_000_000, transcendentals=0),
    )(activations, sketch)
    lower = jnp.linalg.cholesky(gram)
    cross = jnp.concatenate([crossed[0].T, crossed[1].T], axis=0)
    return lax.linalg.triangular_solve(lower, cross, left_side=False, lower=True, transpose_a=True)


def solution(mesh):
    return jax.shard_map(
        local,
        mesh=mesh,
        in_specs=(P(("grp", "lane"), None), P()),
        out_specs=P("lane", None),
        check_vma=False,
    )
```

time: 265 us -> 123 us (0.46)
  waiting for transfers between devices: 165 us -> 0 us
  Pallas kernels: 0 us -> 58.1 us
  matrix products: 22.3 us -> 1.37 us
  between operations: 14.7 us -> 1.4 us
    psum x1 -> x0, waiting for transfers between devices: 165 us -> none  [local(): summed = lax.psum(term, ('grp', 'lane'))]
    pallas_call x0 -> x1, Pallas kernels: none -> 58.1 us  [local(): pl.pallas_call(kernel, out_shape=(jax.ShapeDtypeStruct((2, 256, 128), F32...]
    dot_general x3 -> x0, matrix products: 19.1 us -> none  [the longest x1 9.87 us: local(): sampled = jnp.dot(activations, sketch, preferred_element_type=jnp.float32)]
  transfers between devices with their start and end apart: 1 -> 0, of which waited for: 1 -> 0; matrix products, arithmetic and copies ran while one was open for 0% -> 0% of each run, Pallas kernels for 0% -> 0%
where the time goes in v1:
time: 123 us
  Pallas kernels  58.1 us (47%)
  other arithmetic  54.9 us (45%)
  local copies, waits for them, and re-layouts  7 us (6%)
  between operations  1.4 us (1%)
  matrix products  1.37 us (1%)
    pallas_call x1, Pallas kernels, local(): pl.pallas_call(kernel, out_shape=(jax.ShapeDtypeStruct((2, 256, 128), F32...  58.1 us
    another operation x6, other arithmetic, local(): lower = jnp.linalg.cholesky(gram)  34 us
    another operation x4, other arithmetic, local(): lax.linalg.triangular_solve(lower, cross, left_side=False, lower=True, tr...  19.9 us
    another operation x6, local copies, waits for them, and re-layouts  4 us

profile of v1, /device:TPU:0, one launch (start us, length us, event | category | flops | bytes accessed | tf_op | source)
XLA Modules:
  0.0 122.8 jit_solution(14882330124018065984)
XLA Ops:
  0.0 58.1 %shard_map.28 = (f32[2,256,128]{2,1,0:T(8,128)}, f32[256,256]{1,0:T(8,128)}) custom-call(bf16[1024,8192]{1,0:T(8,128)(2,1)} %a_hbm.1, bf16[8192,256]{1,0:T(8,128)(2,1)} %s_hbm.1), custom_call_target="tpu_custom_call" | custom-call | flops 8999999488 | bytes 22000000 | tf_op jit(solution)/shard_map/pallas_call | solution.py:280
  58.1 1.1 copy.3
  59.2 1.0 fusion
  60.2 11.7 %cholesky.50 = f32[128,128]{1,0:T(8,128)S(1)} custom-call(f32[128,128]{1,0:T(8,128)S(1)} %cholesky.118), custom_call_target="Cholesky" | custom-call | tf_op jit(solution)/shard_map/jit(cholesky)/cholesky | solution.py:298
  71.9 9.8 %custom-call.14 = f32[1,128,128]{1,2,0:T(8,128)S(1)} custom-call(f32[1,128,128]{2,1,0:T(8,128)S(1)} %get-tuple-element.32), custom_call_target="InvertDiagBlocksLowerTriangular" | custom-call | tf_op jit(solution)/shard_map/jit(cholesky)/cholesky | solution.py:298
  81.8 0.2 constant_dynamic-update-slice_fusion.1
  82.0 0.3 convolution_subtract_fusion.1
  82.2 11.7 %cholesky.105 = f32[128,128]{1,0:T(8,128)S(1)} custom-call(f32[128,128]{1,0:T(8,128)S(1)} %convolution_subtract_fusion.1), custom_call_target="Cholesky" | custom-call | tf_op jit(solution)/shard_map/jit(cholesky)/cholesky | solution.py:298
  94.0 0.7 compare_reduce_fusion
  96.0 0.1 triangular_solve.58
  96.1 4.0 %while.1 = (s32[]{:T(128)}, f32[256,256]{1,0:T(8,128)S(1)}, s32[2,2]{1,0:T(2,128)S(1)}, f32[2,128,128]{2,1,0:T(8,128)S(1)}, s32[]{:T(128)}) while((s32[]{:T(128)}, f32[256,256]{1,0:T(8,128)S(1)}, s32[2,2]{1,0:T(2,128)S(1)}, f32[2,128,128]{2,1,0:T(8,128)S(1)}, s32[]{:T(128)}) %tuple.24), condition=%wide.while_cond, body=%wide.while_body.sunk | while | flops 2 | bytes 131181 | solution.py:300
  96.1 0.6 fusion.16
  96.8 1.3 %bitcast_dynamic-update-slice_fusion.2 = f32[2,128,128]{2,1,0:T(8,128)S(1)} fusion(f32[2,128,128]{2,1,0:T(8,128)S(1)} %get-tuple-element.74, s32[]{:T(128)} %get-tuple-element.71, f32[256,256]{1,0:T(8,128)S(1)} %get-tuple-element.77, s32[]{:T(128)} %bitcast.37, s32[]{:T(128)} %bitcast.38), kind=kLoop, calls=%fused_computation.clone.1 | loop fusion | bytes 131084 | tf_op jit(solution)/shard_map/triangular_solve
  98.1 0.6 fusion.16
  98.8 1.3 %bitcast_dynamic-update-slice_fusion.2 = f32[2,128,128]{2,1,0:T(8,128)S(1)} fusion(f32[2,128,128]{2,1,0:T(8,128)S(1)} %get-tuple-element.74, s32[]{:T(128)} %get-tuple-element.71, f32[256,256]{1,0:T(8,128)S(1)} %get-tuple-element.77, s32[]{:T(128)} %bitcast.37, s32[]{:T(128)} %bitcast.38), kind=kLoop, calls=%fused_computation.clone.1 | loop fusion | bytes 131084 | tf_op jit(solution)/shard_map/triangular_solve
  100.1 19.9 %custom-call.15 = f32[2,128,128]{1,2,0:T(8,128)S(1)} custom-call(f32[2,128,128]{2,1,0:T(8,128)S(1)} %get-tuple-element.16), custom_call_target="InvertDiagBlocksLowerTriangular" | custom-call | tf_op jit(solution)/shard_map/triangular_solve | solution.py:300
  120.0 1.0 slice_bitcast_fusion
  121.0 0.3 fusion.2
  121.3 0.3 convolution_subtract_fusion
  121.6 0.3 fusion.4
  121.9 0.8 copy.4
  (10 shorter events, 0.2 us)

commit v2 on v1

--- a/solution.py
+++ b/solution.py
@@ -11,6 +11,7 @@
 F32, BF16 = jnp.float32, jnp.bfloat16
 NK, KW = 8, 1024
 RX, RZ, RY = 80, 80, 96
+NB = 64
 Y0, HXZ, HY, HY1 = RX + RZ, (RX + RZ) // 2, RY // 2, RY // 4
 
 
@@ -22,10 +23,79 @@
     pltpu.make_async_copy(ref, ref, sem).wait()
 
 
+def panel(rows, q):
+    n = len(rows)
+    top = rows[q]
+    wide = top.shape
+    at = 8 * q
+
+    def lanes(v, k):
+        return jnp.broadcast_to(v[:, at + k:at + k + 1], wide)
+
+    def subl(v, k):
+        return jnp.broadcast_to(v[k:k + 1, :], wide)
+
+    cols = [lanes(top, k) for k in range(8)]
+    a = {(l, k): subl(cols[k], l) for k in range(8) for l in range(k, 8)}
+    below = {i: [lanes(rows[i], k) for k in range(8)] for i in range(q + 1, n)}
+    b = [subl(top, k) for k in range(8)]
+    inv = []
+    for k in range(8):
+        rs = lax.rsqrt(a[k, k])
+        inv.append(rs)
+        for l in range(k + 1, 8):
+            a[l, k] = a[l, k] * rs
+        for m in range(k + 1, 8):
+            for l in range(m, 8):
+                a[l, m] = a[l, m] - a[l, k] * a[m, k]
+        b[k] = b[k] * rs
+        for l in range(k + 1, 8):
+            b[l] = b[l] - a[l, k] * b[k]
+    if q + 1 < n:
+        d = [None] * 8
+        for k in reversed(range(8)):
+            v = b[k]
+            for l in range(7, k, -1):
+                v = v - a[l, k] * d[l]
+            d[k] = v * inv[k]
+        for i in range(q + 1, n):
+            v = rows[i]
+            for k in reversed(range(8)):
+                v = v - below[i][k] * d[k]
+            rows[i] = v
+    sub = lax.broadcasted_iota(jnp.int32, wide, 0)
+    out = b[0]
+    for k in range(1, 8):
+        out = jnp.where(sub == k, b[k], out)
+    return out
+
+
+def mm32(u, v):
+    return jnp.dot(u, v, precision=lax.Precision.HIGHEST, preferred_element_type=F32)
+
+
+def factor_step(gm, em, j):
+    lo, hi = j * NB, (j + 1) * NB
+    eye = (
+        lax.broadcasted_iota(jnp.int32, (NB, NB), 0) == lax.broadcasted_iota(jnp.int32, (NB, NB), 1)
+    ).astype(F32)
+    m = jnp.concatenate([gm[lo:hi, lo:hi], eye], axis=1)
+    rows = [m[8 * i : 8 * i + 8, :] for i in range(NB // 8)]
+    w = jnp.concatenate([panel(rows, q) for q in range(NB // 8)], axis=0)[:, NB:]
+    if j:
+        em[lo:hi, 0:lo] = mm32(w, em[lo:hi, 0:lo])
+    em[lo:hi, lo:hi] = w
+    if hi < 256:
+        t = mm32(w, gm[lo:hi, hi:256])
+        tt = t.T
+        gm[hi:256, hi:256] -= mm32(tt, t)
+        em[hi:256, 0:hi] -= mm32(tt, em[lo:hi, 0:hi])
+
+
 def kernel(
-    a_hbm, s_hbm, c_out, g_out,
+    a_hbm, s_hbm, out,
     a, s, acc, ht, g, gh, gr, gy, gf, q, r, p, cb,
-    rx, rz, ry, rx2, rz2, ry1, ry2, rq3, ry13, ry23,
+    rx, rz, ry, rx2, rz2, ry1, ry2, rq3, ry13, ry23, em,
     asem, ssem, gsem, qsem, rsem, ss1, rs1, ss2, rs2, ss3, rs3, ss4, rs4,
 ):
     y, lane = lax.axis_index("grp"), lax.axis_index("lane")
@@ -204,6 +274,12 @@
 
     wait(gf.at[pl.ds(0, 120), :], gsem.at[7])
     send(gf.at[mine, :], gf.at[mine, :], gsem.at[8], gsem.at[9], core)
+    em[...] = jnp.zeros_like(em)
+    wait(gf.at[pl.ds(0, 120), :], gsem.at[6])
+    wait(gf.at[mine, :], gsem.at[8])
+    wait(gf.at[other, :], gsem.at[9])
+    factor_step(gf, em, 0)
+    factor_step(gf, em, 1)
 
     for d in range(3):
         wait(rx2.at[d], rs2.at[d])
@@ -227,6 +303,8 @@
     for d in range(1, 4):
         x_ = mod4(x + d)
         send(p.at[x_, z, ch, rows_2, :], ry23.at[d - 1], ss3.at[5 + d], rs3.at[5 + d], dev(x_, y, z, c))
+
+    factor_step(gf, em, 2)
 
     rows_q = pl.ds(pl.multiple_of(lax.div(y, 2) * HXZ, 8), HXZ)
     for d in range(3):
@@ -242,6 +320,8 @@
     for d in range(1, 4):
         send(cb.at[ch, rows_y, :], cb.at[ch, rows_y, :], ss4.at[d + 2], rs4.at[d + 2], dev(x, mod4(y + d), z, c))
 
+    factor_step(gf, em, 3)
+
     def sent(t, carry):
         x_, z_ = lax.div(t, 4), lax.rem(t, 4)
         wait(q.at[x_, z_], qsem.at[t])
@@ -251,8 +331,6 @@
     wait(gh, gsem.at[0])
     wait(gr, gsem.at[2])
     wait(gy.at[pl.ds(0, 3)], gsem.at[4])
-    wait(gf.at[pl.ds(0, 120), :], gsem.at[6])
-    wait(gf.at[mine, :], gsem.at[8])
     for d in range(3):
         wait(rx.at[d], ss1.at[d])
         wait(rz.at[d], ss1.at[3 + d])
@@ -266,38 +344,34 @@
         wait(ry23.at[d], ss3.at[6 + d])
         wait(rq3.at[d], ss4.at[d])
         wait(cb.at[ch, rows_y, :], ss4.at[3 + d])
-    wait(gf.at[other, :], gsem.at[9])
-    g_out[...] = gf[...]
     for d in range(3):
         wait(rq3.at[d], rs4.at[d])
         wait(cb.at[ch, rows_y, :], rs4.at[3 + d])
-    c_out[...] = cb[...]
+    for h in range(2):
+        out[128 * h : 128 * h + 128, :] = mm32(em[...], cb[h]).T
 
 
 def local(activations, sketch):
     dma = pltpu.SemaphoreType.DMA
     vmem = pltpu.VMEM
-    crossed, gram = pl.pallas_call(
+    return pl.pallas_call(
         kernel,
-        out_shape=(jax.ShapeDtypeStruct((2, 256, 128), F32), jax.ShapeDtypeStruct((256, 256), F32)),
+        out_shape=jax.ShapeDtypeStruct((256, 256), F32),
         in_specs=[pl.BlockSpec(memory_space=pl.ANY)] * 2,
-        out_specs=[pl.BlockSpec(memory_space=pltpu.VMEM)] * 2,
+        out_specs=pl.BlockSpec(memory_space=pltpu.VMEM),
         scratch_shapes=[
             vmem((1024, 8192), BF16), vmem((8192, 256), BF16), vmem((1024, 256), F32), vmem((256, 1024), BF16),
             vmem((256, 256), F32), vmem((128, 256), F32), vmem((15, 8, 256), F32), vmem((4, 8, 256), F32), vmem((256, 256), F32),
             vmem((4, 4, 2, 256, 128), F32), vmem((4, 4, 2, 256, 128), F32), vmem((4, 4, 2, 256, 128), F32), vmem((2, 256, 128), F32),
             vmem((3, 4, 2, RX, 128), F32), vmem((3, 4, 2, RZ, 128), F32), vmem((3, 4, 4, HY, 128), F32),
             vmem((3, 2, RX, 128), F32), vmem((3, 2, RZ, 128), F32), vmem((3, 4, HY1, 128), F32), vmem((3, 4, HY - HY1, 128), F32),
-            vmem((3, HXZ, 128), F32), vmem((3, HY1, 128), F32), vmem((3, HY - HY1, 128), F32),
+            vmem((3, HXZ, 128), F32), vmem((3, HY1, 128), F32), vmem((3, HY - HY1, 128), F32), vmem((256, 256), F32),
             dma((NK,)), dma((NK,)), dma((10,)), dma((16,)), dma((16,)),
             dma((9,)), dma((9,)), dma((12,)), dma((12,)), dma((9,)), dma((9,)), dma((6,)), dma((6,)),
         ],
         compiler_params=pltpu.CompilerParams(collective_id=0, has_side_effects=True, vmem_limit_bytes=56 << 20),
         cost_estimate=pl.CostEstimate(flops=9_000_000_000, bytes_accessed=22_000_000, transcendentals=0),
     )(activations, sketch)
-    lower = jnp.linalg.cholesky(gram)
-    cross = jnp.concatenate([crossed[0].T, crossed[1].T], axis=0)
-    return lax.linalg.triangular_solve(lower, cross, left_side=False, lower=True, transpose_a=True)
 
 
 def solution(mesh):

time: 123 us -> 67.3 us (0.55)
  other arithmetic: 54.9 us -> 0 us
  Pallas kernels: 58.1 us -> 65.4 us
  local copies, waits for them, and re-layouts: 7 us -> 1.67 us
  between operations: 1.4 us -> 0.01 us
  matrix products: 1.37 us -> 0 us
    another operation x10 -> x0, other arithmetic: 53.9 us -> none  [the longest x6 34 us: local(): lower = jnp.linalg.cholesky(gram)]
    pallas_call x1, Pallas kernels: 58.1 us -> 65.4 us  [local(): pl.pallas_call(kernel, out_shape=jax.ShapeDtypeStruct((256, 256), F32), i...]
    another operation x10 -> x0, local copies, waits for them, and re-layouts: 4.93 us -> none
    unnamed x0 -> x1, local copies, waits for them, and re-layouts: none -> 1.67 us
    another operation x5 -> x0, matrix products: 1.37 us -> none  [the longest x3 0.9 us: local(): lax.linalg.triangular_solve(lower, cross, left_side=False, lower=True, tr...]
where the time goes in v2:
time: 67.3 us; the launch traced here: 67.1 us
  Pallas kernels  65.4 us (97%)
  local copies, waits for them, and re-layouts  1.67 us (2%)
    pallas_call x1, Pallas kernels, local(): pl.pallas_call(kernel, out_shape=jax.ShapeDtypeStruct((256, 256), F32), i...  65.4 us
    unnamed x1, local copies, waits for them, and re-layouts  1.67 us

profile of v2, /device:TPU:0, one launch (start us, length us, event | category | flops | bytes accessed | tf_op | source)
XLA Modules:
  0.0 67.1 jit_solution(17741400816063046247)
XLA Ops:
  0.0 65.4 %shard_map.28 = f32[256,256]{1,0:T(8,128)} custom-call(bf16[1024,8192]{1,0:T(8,128)(2,1)} %a_hbm.1, bf16[8192,256]{1,0:T(8,128)(2,1)} %s_hbm.1), custom_call_target="tpu_custom_call" | custom-call | flops 8999999488 | bytes 22000000 | tf_op jit(solution)/shard_map/pallas_call | solution.py:357
  65.4 1.7 %copy.4 = f32[256,256]{1,0:T(8,128)} copy(f32[256,256]{1,0:T(8,128)} %shard_map.28) | data formatting | bytes 524288

commit v3 on v2

--- a/solution.py
+++ b/solution.py
@@ -12,7 +12,7 @@
 NK, KW = 8, 1024
 RX, RZ, RY = 80, 80, 96
 NB = 64
-Y0, HXZ, HY, HY1 = RX + RZ, (RX + RZ) // 2, RY // 2, RY // 4
+Y0, HXZ, HY, HY1 = RX + RZ, (RX + RZ) // 2, RY // 2, 24
 
 
 def mod4(v):
@@ -110,7 +110,7 @@
         ).start()
 
     def load(i):
-        cols = pl.ds(i * KW, KW)
+        cols = pl.ds(pl.multiple_of(i * KW, KW), KW)
         return (
             pltpu.make_async_copy(s_hbm.at[cols, :], s.at[cols, :], ssem.at[i]),
             pltpu.make_async_copy(a_hbm.at[:, cols], a.at[:, cols], asem.at[i]),
@@ -136,16 +136,10 @@
 
     def sample(i, carry):
         cols = pl.ds(pl.multiple_of(i * KW, KW), KW)
-        for copy in load_dyn(cols, i):
+        for copy in load(i):
             copy.wait()
         acc[...] += jnp.dot(a[:, cols], s[cols, :], preferred_element_type=F32)
         return carry
-
-    def load_dyn(cols, i):
-        return (
-            pltpu.make_async_copy(s_hbm.at[cols, :], s.at[cols, :], ssem.at[i]),
-            pltpu.make_async_copy(a_hbm.at[:, cols], a.at[:, cols], asem.at[i]),
-        )
 
     lax.fori_loop(0, NK, sample, 0)
 
@@ -175,73 +169,127 @@
     core = dev(x, y, z, 1 - c)
     send(g.at[other, :], gh, gsem.at[0], gsem.at[1], core)
 
-    def order(t):
-        dx, dz = mod4(t + 1), mod4(lax.div(t, 4) + t + 1)
+    def piece(x_, z_):
+        return pl.ds(pl.multiple_of(c * 128 + (x_ * 4 + z_) * 8, 8), 8)
+
+    def plane(d):
+        return mod4(x + lax.div(d, 4)), mod4(z + lax.rem(d, 4))
+
+    def scatter_gram(d, carry):
+        x_, z_ = plane(d)
+        send(g.at[piece(x_, z_), :], gr.at[d - 1], gsem.at[2], gsem.at[3], dev(x_, y, z_, c))
+        return carry
+
+    def order(i, k):
+        dx, dz = (k + 1) % 4, mod4(i + k + 1)
         return dx, dz, mod4(x + dx), mod4(z + dz)
 
     def block(x_, z_, c_):
         lb = (x_ * 4 + z_) * 2 + c_
         return mm(ht[...], a[:, pl.ds(pl.multiple_of(lb * 256, 256), 256)])
 
-    def give(t, carry):
-        _, _, x_, z_ = order(t)
-        b = block(x_, z_, 1 - c)
-        q[x_, z_, 0] = b[:, :128]
-        q[x_, z_, 1] = b[:, 128:]
-        send(q.at[x_, z_], r.at[x_, z_], qsem.at[x_ * 4 + z_], rsem.at[x_ * 4 + z_], core)
-        return carry
-
-    lax.fori_loop(0, 16, give, 0)
-
-    wait(gh, gsem.at[1])
-    g[mine, :] += gh[...]
-
-    def piece(x_, z_):
-        return pl.ds(pl.multiple_of(c * 128 + (x_ * 4 + z_) * 8, 8), 8)
-
-    def scatter_gram(d, carry):
-        x_, z_ = mod4(x + lax.div(d, 4)), mod4(z + lax.rem(d, 4))
-        send(g.at[piece(x_, z_), :], gr.at[d - 1], gsem.at[2], gsem.at[3], dev(x_, y, z_, c))
-        return carry
-
-    lax.fori_loop(1, 16, scatter_gram, 0)
-
-    def own(t, carry):
-        dx, dz, x_, z_ = order(t)
-        b = block(x_, z_, c)
-        wait(r.at[x_, z_], rsem.at[x_ * 4 + z_])
-        p[x_, z_, 0] = b[:, :128] + r[x_, z_, 0]
-        p[x_, z_, 1] = b[:, 128:] + r[x_, z_, 1]
-
-        @pl.when(dx != 0)
+    def give(i):
+        for k in range(4):
+            _, _, x_, z_ = order(i, k)
+            b = block(x_, z_, 1 - c)
+            q[x_, z_, 0] = b[:, :128]
+            q[x_, z_, 1] = b[:, 128:]
+        for k in range(4):
+            _, _, x_, z_ = order(i, k)
+            send(q.at[x_, z_], r.at[x_, z_], qsem.at[x_ * 4 + z_], rsem.at[x_ * 4 + z_], core)
+
+    def own(i):
+        for k in range(4):
+            _, _, x_, z_ = order(i, k)
+            b = block(x_, z_, c)
+            p[x_, z_, 0] = b[:, :128]
+            p[x_, z_, 1] = b[:, 128:]
+        for k in range(4):
+            _, _, x_, z_ = order(i, k)
+            wait(r.at[x_, z_], rsem.at[x_ * 4 + z_])
+            p[x_, z_] += r[x_, z_]
+
+    def scatter(i):
+        for k in range(4):
+            dx, dz, x_, z_ = order(i, k)
+            if dx:
+                send(p.at[x_, z_, :, pl.ds(0, RX), :], rx.at[dx - 1, z_], ss1.at[dx - 1], rs1.at[dx - 1], dev(x_, y, z, c))
+
+            @pl.when(dz != 0)
+            def _():
+                send(p.at[x_, z_, :, pl.ds(RX, RZ), :], rz.at[dz - 1, x_], ss1.at[dz + 2], rs1.at[dz + 2], dev(x, y, z_, c))
+
+            for d in range(1, 4):
+                y_ = mod4(y + d)
+                rows = pl.ds(pl.multiple_of(Y0 + lax.div(y_, 2) * HY, 8), HY)
+                send(p.at[x_, z_, lax.rem(y_, 2), rows, :], ry.at[d - 1, x_, z_], ss1.at[5 + d], rs1.at[5 + d], dev(x, y_, z, c))
+
+    def turn(i, carry):
+        @pl.when(i < 4)
         def _():
-            send(p.at[x_, z_, :, pl.ds(0, RX), :], rx.at[dx - 1, z_], ss1.at[dx - 1], rs1.at[dx - 1], dev(x_, y, z, c))
-
-        @pl.when(dz != 0)
+            give(i)
+
+        @pl.when(i == 1)
         def _():
-            send(p.at[x_, z_, :, pl.ds(RX, RZ), :], rz.at[dz - 1, x_], ss1.at[dz + 2], rs1.at[dz + 2], dev(x, y, z_, c))
-
-        for d in range(1, 4):
-            y_ = mod4(y + d)
-            rows = pl.ds(pl.multiple_of(Y0 + lax.div(y_, 2) * HY, 8), HY)
-            send(p.at[x_, z_, lax.rem(y_, 2), rows, :], ry.at[d - 1, x_, z_], ss1.at[5 + d], rs1.at[5 + d], dev(x, y_, z, c))
-        return carry
-
-    lax.fori_loop(0, 16, own, 0)
-
-    wait(gr, gsem.at[3])
-    gy[y] = g[piece(x, z), :] + jnp.sum(gr[...], axis=0)
-    for d in range(1, 4):
-        send(gy.at[y], gy.at[y], gsem.at[4], gsem.at[5], dev(x, mod4(y + d), z, c))
-    wait(gy.at[pl.ds(0, 3)], gsem.at[5])
-    gf[piece(x, z), :] = (gy[0] + gy[1]) + (gy[2] + gy[3])
+            wait(gh, gsem.at[1])
+            g[mine, :] += gh[...]
+            lax.fori_loop(1, 16, scatter_gram, 0)
+
+        @pl.when(i == 4)
+        def _():
+            wait(gr, gsem.at[3])
+            gy[y] = g[piece(x, z), :] + jnp.sum(gr[...], axis=0)
+            for d in range(1, 4):
+                send(gy.at[y], gy.at[y], gsem.at[4], gsem.at[5], dev(x, mod4(y + d), z, c))
+            scatter(1)
+
+        @pl.when(i >= 1)
+        def _():
+            own(i - 1)
+
+        @pl.when(i == 1)
+        def _():
+            scatter(0)
+
+        return carry
+
+    lax.fori_loop(0, 5, turn, 0)
 
     def gather_gram(d, carry):
-        x_, z_ = mod4(x + lax.div(d, 4)), mod4(z + lax.rem(d, 4))
+        x_, z_ = plane(d)
         send(gf.at[piece(x, z), :], gf.at[piece(x, z), :], gsem.at[6], gsem.at[7], dev(x_, y, z_, c))
         return carry
 
-    lax.fori_loop(1, 16, gather_gram, 0)
+    def rest(i, carry):
+        scatter(i)
+        return carry
+
+    def sum_groups():
+        wait(gy.at[pl.ds(0, 3)], gsem.at[5])
+        gf[piece(x, z), :] = (gy[0] + gy[1]) + (gy[2] + gy[3])
+        lax.fori_loop(1, 16, gather_gram, 0)
+        lax.fori_loop(2, 4, rest, 0)
+
+    def swap_halves():
+        wait(gf.at[pl.ds(0, 120), :], gsem.at[7])
+        send(gf.at[mine, :], gf.at[mine, :], gsem.at[8], gsem.at[9], core)
+        em[...] = jnp.zeros_like(em)
+
+    def halves():
+        wait(gf.at[pl.ds(0, 120), :], gsem.at[6])
+        wait(gf.at[mine, :], gsem.at[8])
+        wait(gf.at[other, :], gsem.at[9])
+
+    def f(j):
+        return lambda: factor_step(gf, em, j)
+
+    plan = {0: (sum_groups, swap_halves, halves, f(0)), 1: (f(1),), 2: (f(2),), 3: (f(3),), 4: ()}
+
+    def slot(i):
+        for step in plan[i]:
+            step()
+
+    slot(0)
 
     ch = lax.rem(y, 2)
     y0 = Y0 + lax.div(y, 2) * HY
@@ -263,6 +311,7 @@
     for d in range(1, 4):
         x_ = mod4(x + d)
         send(p.at[x_, z, :, rows_z, :], rz2.at[d - 1], ss2.at[2 + d], rs2.at[2 + d], dev(x_, y, z, c))
+    slot(1)
     for d in range(3):
         wait(ry.at[d], rs1.at[6 + d])
     for k in range(4):
@@ -272,14 +321,7 @@
         send(p.at[x_, :, ch, rows_1, :], ry1.at[d - 1], ss2.at[5 + d], rs2.at[5 + d], dev(x_, y, z, c))
         send(p.at[:, z_, ch, rows_2, :], ry2.at[d - 1], ss2.at[8 + d], rs2.at[8 + d], dev(x, y, z_, c))
 
-    wait(gf.at[pl.ds(0, 120), :], gsem.at[7])
-    send(gf.at[mine, :], gf.at[mine, :], gsem.at[8], gsem.at[9], core)
-    em[...] = jnp.zeros_like(em)
-    wait(gf.at[pl.ds(0, 120), :], gsem.at[6])
-    wait(gf.at[mine, :], gsem.at[8])
-    wait(gf.at[other, :], gsem.at[9])
-    factor_step(gf, em, 0)
-    factor_step(gf, em, 1)
+    slot(2)
 
     for d in range(3):
         wait(rx2.at[d], rs2.at[d])
@@ -304,7 +346,7 @@
         x_ = mod4(x + d)
         send(p.at[x_, z, ch, rows_2, :], ry23.at[d - 1], ss3.at[5 + d], rs3.at[5 + d], dev(x_, y, z, c))
 
-    factor_step(gf, em, 2)
+    slot(3)
 
     rows_q = pl.ds(pl.multiple_of(lax.div(y, 2) * HXZ, 8), HXZ)
     for d in range(3):
@@ -320,7 +362,7 @@
     for d in range(1, 4):
         send(cb.at[ch, rows_y, :], cb.at[ch, rows_y, :], ss4.at[d + 2], rs4.at[d + 2], dev(x, mod4(y + d), z, c))
 
-    factor_step(gf, em, 3)
+    slot(4)
 
     def sent(t, carry):
         x_, z_ = lax.div(t, 4), lax.rem(t, 4)
@@ -348,7 +390,7 @@
         wait(rq3.at[d], rs4.at[d])
         wait(cb.at[ch, rows_y, :], rs4.at[3 + d])
     for h in range(2):
-        out[128 * h : 128 * h + 128, :] = mm32(em[...], cb[h]).T
+        out[:, 128 * h : 128 * h + 128] = mm32(em[...], cb[h])
 
 
 def local(activations, sketch):
@@ -371,7 +413,7 @@
         ],
         compiler_params=pltpu.CompilerParams(collective_id=0, has_side_effects=True, vmem_limit_bytes=56 << 20),
         cost_estimate=pl.CostEstimate(flops=9_000_000_000, bytes_accessed=22_000_000, transcendentals=0),
-    )(activations, sketch)
+    )(activations, sketch).T
 
 
 def solution(mesh):

time: 67.3 us -> 56.5 us (0.84)
  Pallas kernels: 65.4 us -> 54.5 us
    pallas_call x1, Pallas kernels: 65.4 us -> 54.5 us  [local(): pl.pallas_call(kernel, out_shape=jax.ShapeDtypeStruct((256, 256), F32), i...]
    transpose x0 -> x1, local copies, waits for them, and re-layouts: none -> 1.79 us  [local(): return pl.pallas_call(kernel, out_shape=jax.ShapeDtypeStruct((256, 256),...]
    unnamed x1 -> x0, local copies, waits for them, and re-layouts: 1.67 us -> none
where the time goes in v3:
time: 56.5 us; the launch traced here: 56.3 us
  Pallas kernels  54.5 us (96%)
  local copies, waits for them, and re-layouts  1.79 us (3%)
    pallas_call x1, Pallas kernels, local(): pl.pallas_call(kernel, out_shape=jax.ShapeDtypeStruct((256, 256), F32), i...  54.5 us
    transpose x1, local copies, waits for them, and re-layouts, local(): return pl.pallas_call(kernel, out_shape=jax.ShapeDtypeStruct((256, 256),...  1.79 us

profile of v3, /device:TPU:0, one launch (start us, length us, event | category | flops | bytes accessed | tf_op | source)
XLA Modules:
  0.0 56.3 jit_solution(16482754607330668804)
XLA Ops:
  0.0 54.5 %shard_map.28 = f32[256,256]{1,0:T(8,128)} custom-call(bf16[1024,8192]{1,0:T(8,128)(2,1)} %a_hbm.1, bf16[8192,256]{1,0:T(8,128)(2,1)} %s_hbm.1), custom_call_target="tpu_custom_call" | custom-call | flops 8999999488 | bytes 22000000 | tf_op jit(solution)/shard_map/pallas_call | solution.py:399
  54.5 1.8 %copy.3 = f32[256,256]{1,0:T(8,128)} copy(f32[256,256]{0,1:T(8,128)} %bitcast.1) | data formatting | bytes 524288 | tf_op jit(solution)/shard_map/transpose | solution.py:416

commit v4 on v3

--- a/solution.py
+++ b/solution.py
@@ -95,8 +95,8 @@
 def kernel(
     a_hbm, s_hbm, out,
     a, s, acc, ht, g, gh, gr, gy, gf, q, r, p, cb,
-    rx, rz, ry, rx2, rz2, ry1, ry2, rq3, ry13, ry23, em,
-    asem, ssem, gsem, qsem, rsem, ss1, rs1, ss2, rs2, ss3, rs3, ss4, rs4,
+    qx, qz, qy, rx, rz, ry, rx2, rz2, ry1, ry2, rq3, ry13, ry23, em,
+    asem, ssem, gsem, qsem, rsem, ss0, xs0, zs0, ys0, ss1, rs1, ss2, rs2, ss3, rs3, ss4, rs4,
 ):
     y, lane = lax.axis_index("grp"), lax.axis_index("lane")
     x, z, c = lax.div(lane, 8), mod4(lax.div(lane, 2)), lax.rem(lane, 2)
@@ -209,20 +209,79 @@
             wait(r.at[x_, z_], rsem.at[x_ * 4 + z_])
             p[x_, z_] += r[x_, z_]
 
+    half_x, half_z = (pl.ds(0, RX), pl.ds(RX, RZ))
+
+    def quarter(y_):
+        return lax.rem(y_, 2), pl.ds(pl.multiple_of(Y0 + lax.div(y_, 2) * HY, 8), HY)
+
+    def to_x(z_, h, way):
+        x_ = mod4(x + 1 + 2 * way)
+        send(p.at[x_, z_, h, half_x, :], rx.at[way, z_, h], ss1.at[0], rs1.at[way], dev(x_, y, z, c))
+
+    def to_z(x_, h, way):
+        z_ = mod4(z + 1 + 2 * way)
+        send(p.at[x_, z_, h, half_z, :], rz.at[way, x_, h], ss1.at[1], rs1.at[2 + way], dev(x, y, z_, c))
+
+    def to_y(x_, z_, way):
+        y_ = mod4(y + 1 + 2 * way)
+        ch_, rows = quarter(y_)
+        send(p.at[x_, z_, ch_, rows, :], ry.at[way, x_, z_], ss1.at[2], rs1.at[4 + way], dev(x, y_, z, c))
+
     def scatter(i):
         for k in range(4):
             dx, dz, x_, z_ = order(i, k)
-            if dx:
-                send(p.at[x_, z_, :, pl.ds(0, RX), :], rx.at[dx - 1, z_], ss1.at[dx - 1], rs1.at[dx - 1], dev(x_, y, z, c))
-
-            @pl.when(dz != 0)
+            way_y = k // 2
+            ch_, rows = quarter(mod4(y + 2))
+            send(p.at[x_, z_, ch_, rows, :], qy.at[x_, z_], ss0.at[2], ys0.at[x_ * 4 + z_], dev(x, mod4(y + 1 + 2 * way_y), z, c))
+            if dx == 2:
+                for way in range(2):
+                    to = dev(mod4(x + 1 + 2 * way), y, z, c)
+                    send(p.at[x_, z_, way, half_x, :], qx.at[way, z_], ss0.at[0], xs0.at[way * 4 + z_], to)
+
+            @pl.when(dz == 2)
             def _():
-                send(p.at[x_, z_, :, pl.ds(RX, RZ), :], rz.at[dz - 1, x_], ss1.at[dz + 2], rs1.at[dz + 2], dev(x, y, z_, c))
-
-            for d in range(1, 4):
-                y_ = mod4(y + d)
-                rows = pl.ds(pl.multiple_of(Y0 + lax.div(y_, 2) * HY, 8), HY)
-                send(p.at[x_, z_, lax.rem(y_, 2), rows, :], ry.at[d - 1, x_, z_], ss1.at[5 + d], rs1.at[5 + d], dev(x, y_, z, c))
+                for way in range(2):
+                    to = dev(x, y, mod4(z + 1 + 2 * way), c)
+                    send(p.at[x_, z_, way, half_z, :], qz.at[way, x_], ss0.at[1], zs0.at[way * 4 + x_], to)
+
+        for k in range(4):
+            dx, dz, x_, z_ = order(i, k)
+            to_y(x_, z_, 1 - k // 2)
+            if dx == 1 or dx == 3:
+                to_x(z_, 1 - dx // 2, dx // 2)
+
+            @pl.when(dz == 1)
+            def _():
+                to_z(x_, 1, 0)
+
+            @pl.when(dz == 3)
+            def _():
+                to_z(x_, 0, 1)
+
+    def relay(i, carry):
+        for k in range(4):
+            dx, dz, x_, z_ = order(i, k)
+            if dx == 2:
+                for way in range(2):
+                    x_n = mod4(x + 1 + 2 * way)
+                    wait(qx.at[way, z_], xs0.at[way * 4 + z_])
+                    p[x_n, z_, way, half_x, :] += qx[way, z_]
+                    to_x(z_, way, way)
+
+            @pl.when(dz == 2)
+            def _():
+                for way in range(2):
+                    z_n = mod4(z + 1 + 2 * way)
+                    wait(qz.at[way, x_], zs0.at[way * 4 + x_])
+                    p[x_, z_n, way, half_z, :] += qz[way, x_]
+                    to_z(x_, way, way)
+
+            way_y = k // 2
+            ch_, rows = quarter(mod4(y + 1 + 2 * way_y))
+            wait(qy.at[x_, z_], ys0.at[x_ * 4 + z_])
+            p[x_, z_, ch_, rows, :] += qy[x_, z_]
+            to_y(x_, z_, way_y)
+        return carry
 
     def turn(i, carry):
         @pl.when(i < 4)
@@ -241,15 +300,15 @@
             gy[y] = g[piece(x, z), :] + jnp.sum(gr[...], axis=0)
             for d in range(1, 4):
                 send(gy.at[y], gy.at[y], gsem.at[4], gsem.at[5], dev(x, mod4(y + d), z, c))
-            scatter(1)
+            scatter(2)
 
         @pl.when(i >= 1)
         def _():
             own(i - 1)
 
-        @pl.when(i == 1)
+        @pl.when((i == 1) | (i == 2) | (i == 4))
         def _():
-            scatter(0)
+            scatter(i - 1)
 
         return carry
 
@@ -258,17 +317,13 @@
     def gather_gram(d, carry):
         x_, z_ = plane(d)
         send(gf.at[piece(x, z), :], gf.at[piece(x, z), :], gsem.at[6], gsem.at[7], dev(x_, y, z_, c))
-        return carry
-
-    def rest(i, carry):
-        scatter(i)
         return carry
 
     def sum_groups():
         wait(gy.at[pl.ds(0, 3)], gsem.at[5])
         gf[piece(x, z), :] = (gy[0] + gy[1]) + (gy[2] + gy[3])
         lax.fori_loop(1, 16, gather_gram, 0)
-        lax.fori_loop(2, 4, rest, 0)
+        lax.fori_loop(0, 4, relay, 0)
 
     def swap_halves():
         wait(gf.at[pl.ds(0, 120), :], gsem.at[7])
@@ -283,7 +338,7 @@
     def f(j):
         return lambda: factor_step(gf, em, j)
 
-    plan = {0: (sum_groups, swap_halves, halves, f(0)), 1: (f(1),), 2: (f(2),), 3: (f(3),), 4: ()}
+    plan = {0: (sum_groups, swap_halves), 1: (), 2: (halves, f(0), f(1)), 3: (f(2),), 4: (f(3),)}
 
     def slot(i):
         for step in plan[i]:
@@ -297,25 +352,25 @@
     rows_1 = pl.ds(pl.multiple_of(y0, 8), HY1)
     rows_2 = pl.ds(pl.multiple_of(y0 + HY1, 8), HY - HY1)
     rows_x, rows_z = pl.ds(0, RX), pl.ds(RX, RZ)
-    for d in range(3):
+    for d in range(2):
         wait(rx.at[d], rs1.at[d])
     for k in range(4):
-        p[x, k, :, rows_x, :] += rx[0, k] + rx[1, k] + rx[2, k]
+        p[x, k, :, rows_x, :] += rx[0, k] + rx[1, k]
     for d in range(1, 4):
         z_ = mod4(z + d)
         send(p.at[x, z_, :, rows_x, :], rx2.at[d - 1], ss2.at[d - 1], rs2.at[d - 1], dev(x, y, z_, c))
-    for d in range(3):
-        wait(rz.at[d], rs1.at[3 + d])
+    for d in range(2):
+        wait(rz.at[d], rs1.at[2 + d])
     for k in range(4):
-        p[k, z, :, rows_z, :] += rz[0, k] + rz[1, k] + rz[2, k]
+        p[k, z, :, rows_z, :] += rz[0, k] + rz[1, k]
     for d in range(1, 4):
         x_ = mod4(x + d)
         send(p.at[x_, z, :, rows_z, :], rz2.at[d - 1], ss2.at[2 + d], rs2.at[2 + d], dev(x_, y, z, c))
     slot(1)
-    for d in range(3):
-        wait(ry.at[d], rs1.at[6 + d])
+    for d in range(2):
+        wait(ry.at[d], rs1.at[4 + d])
     for k in range(4):
-        p[k, :, ch, rows_y, :] += ry[0, k] + ry[1, k] + ry[2, k]
+        p[k, :, ch, rows_y, :] += ry[0, k] + ry[1, k]
     for d in range(1, 4):
         x_, z_ = mod4(x + d), mod4(z + d)
         send(p.at[x_, :, ch, rows_1, :], ry1.at[d - 1], ss2.at[5 + d], rs2.at[5 + d], dev(x_, y, z, c))
@@ -370,13 +425,13 @@
         return carry
 
     lax.fori_loop(0, 16, sent, 0)
+    for k, (near, far) in enumerate(((rx, qx), (rz, qz), (ry, qy))):
+        wait(far, ss0.at[k])
+        wait(near, ss1.at[k])
     wait(gh, gsem.at[0])
     wait(gr, gsem.at[2])
     wait(gy.at[pl.ds(0, 3)], gsem.at[4])
     for d in range(3):
-        wait(rx.at[d], ss1.at[d])
-        wait(rz.at[d], ss1.at[3 + d])
-        wait(ry.at[d], ss1.at[6 + d])
         wait(rx2.at[d], ss2.at[d])
         wait(rz2.at[d], ss2.at[3 + d])
         wait(ry1.at[d], ss2.at[6 + d])
@@ -405,11 +460,12 @@
             vmem((1024, 8192), BF16), vmem((8192, 256), BF16), vmem((1024, 256), F32), vmem((256, 1024), BF16),
             vmem((256, 256), F32), vmem((128, 256), F32), vmem((15, 8, 256), F32), vmem((4, 8, 256), F32), vmem((256, 256), F32),
             vmem((4, 4, 2, 256, 128), F32), vmem((4, 4, 2, 256, 128), F32), vmem((4, 4, 2, 256, 128), F32), vmem((2, 256, 128), F32),
-            vmem((3, 4, 2, RX, 128), F32), vmem((3, 4, 2, RZ, 128), F32), vmem((3, 4, 4, HY, 128), F32),
+            vmem((2, 4, RX, 128), F32), vmem((2, 4, RZ, 128), F32), vmem((4, 4, HY, 128), F32),
+            vmem((2, 4, 2, RX, 128), F32), vmem((2, 4, 2, RZ, 128), F32), vmem((2, 4, 4, HY, 128), F32),
             vmem((3, 2, RX, 128), F32), vmem((3, 2, RZ, 128), F32), vmem((3, 4, HY1, 128), F32), vmem((3, 4, HY - HY1, 128), F32),
             vmem((3, HXZ, 128), F32), vmem((3, HY1, 128), F32), vmem((3, HY - HY1, 128), F32), vmem((256, 256), F32),
             dma((NK,)), dma((NK,)), dma((10,)), dma((16,)), dma((16,)),
-            dma((9,)), dma((9,)), dma((12,)), dma((12,)), dma((9,)), dma((9,)), dma((6,)), dma((6,)),
+            dma((3,)), dma((8,)), dma((8,)), dma((16,)), dma((3,)), dma((6,)), dma((12,)), dma((12,)), dma((9,)), dma((9,)), dma((6,)), dma((6,)),
         ],
         compiler_params=pltpu.CompilerParams(collective_id=0, has_side_effects=True, vmem_limit_bytes=56 << 20),
         cost_estimate=pl.CostEstimate(flops=9_000_000_000, bytes_accessed=22_000_000, transcendentals=0),

time: 56.5 us -> 53.3 us (0.943)
  Pallas kernels: 54.5 us -> 51.4 us
    pallas_call x1, Pallas kernels: 54.5 us -> 51.4 us  [local(): pl.pallas_call(kernel, out_shape=jax.ShapeDtypeStruct((256, 256), F32), i...]
where the time goes in v4:
time: 53.3 us; the launch traced here: 53.2 us
  Pallas kernels  51.4 us (96%)
  local copies, waits for them, and re-layouts  1.79 us (3%)
    pallas_call x1, Pallas kernels, local(): pl.pallas_call(kernel, out_shape=jax.ShapeDtypeStruct((256, 256), F32), i...  51.4 us
    transpose x1, local copies, waits for them, and re-layouts, local(): return pl.pallas_call(kernel, out_shape=jax.ShapeDtypeStruct((256, 256),...  1.79 us

profile of v4, /device:TPU:0, one launch (start us, length us, event | category | flops | bytes accessed | tf_op | source)
XLA Modules:
  0.0 53.2 jit_solution(16365557082727146368)
XLA Ops:
  0.0 51.4 %shard_map.28 = f32[256,256]{1,0:T(8,128)} custom-call(bf16[1024,8192]{1,0:T(8,128)(2,1)} %a_hbm.1, bf16[8192,256]{1,0:T(8,128)(2,1)} %s_hbm.1), custom_call_target="tpu_custom_call" | custom-call | flops 8999999488 | bytes 22000000 | tf_op jit(solution)/shard_map/pallas_call | solution.py:454
  51.4 1.8 %copy.3 = f32[256,256]{1,0:T(8,128)} copy(f32[256,256]{0,1:T(8,128)} %bitcast.1) | data formatting | bytes 524288 | tf_op jit(solution)/shard_map/transpose | solution.py:472

commit v5 on v4

--- a/solution.py
+++ b/solution.py
@@ -12,7 +12,8 @@
 NK, KW = 8, 1024
 RX, RZ, RY = 80, 80, 96
 NB = 64
-Y0, HXZ, HY, HY1 = RX + RZ, (RX + RZ) // 2, RY // 2, 24
+RS = 32
+Y0, HXZ, HS, HY, HY1 = RX + RZ, (RX + RZ) // 2 - RS, RS // 2, RY // 2, 24
 
 
 def mod4(v):
@@ -95,7 +96,7 @@
 def kernel(
     a_hbm, s_hbm, out,
     a, s, acc, ht, g, gh, gr, gy, gf, q, r, p, cb,
-    qx, qz, qy, rx, rz, ry, rx2, rz2, ry1, ry2, rq3, ry13, ry23, em,
+    qx, qz, qy, rx, rz, ry, rx2, rz2, ry1, ry2, rq3, ry13, ry23, rxy, rzy, rxy3, rzy3, em,
     asem, ssem, gsem, qsem, rsem, ss0, xs0, zs0, ys0, ss1, rs1, ss2, rs2, ss3, rs3, ss4, rs4,
 ):
     y, lane = lax.axis_index("grp"), lax.axis_index("lane")
@@ -227,7 +228,7 @@
         ch_, rows = quarter(y_)
         send(p.at[x_, z_, ch_, rows, :], ry.at[way, x_, z_], ss1.at[2], rs1.at[4 + way], dev(x, y_, z, c))
 
-    def scatter(i):
+    def scatter_far(i):
         for k in range(4):
             dx, dz, x_, z_ = order(i, k)
             way_y = k // 2
@@ -244,6 +245,7 @@
                     to = dev(x, y, mod4(z + 1 + 2 * way), c)
                     send(p.at[x_, z_, way, half_z, :], qz.at[way, x_], ss0.at[1], zs0.at[way * 4 + x_], to)
 
+    def scatter_near(i):
         for k in range(4):
             dx, dz, x_, z_ = order(i, k)
             to_y(x_, z_, 1 - k // 2)
@@ -283,6 +285,10 @@
             to_y(x_, z_, way_y)
         return carry
 
+    def near(i, carry):
+        scatter_near(i)
+        return carry
+
     def turn(i, carry):
         @pl.when(i < 4)
         def _():
@@ -300,19 +306,22 @@
             gy[y] = g[piece(x, z), :] + jnp.sum(gr[...], axis=0)
             for d in range(1, 4):
                 send(gy.at[y], gy.at[y], gsem.at[4], gsem.at[5], dev(x, mod4(y + d), z, c))
-            scatter(2)
+            scatter_near(1)
 
         @pl.when(i >= 1)
         def _():
             own(i - 1)
 
-        @pl.when((i == 1) | (i == 2) | (i == 4))
+            scatter_far(i - 1)
+
+        @pl.when(i == 2)
         def _():
-            scatter(i - 1)
+            scatter_near(0)
 
         return carry
 
     lax.fori_loop(0, 5, turn, 0)
+    lax.fori_loop(2, 4, near, 0)
 
     def gather_gram(d, carry):
         x_, z_ = plane(d)
@@ -352,20 +361,28 @@
     rows_1 = pl.ds(pl.multiple_of(y0, 8), HY1)
     rows_2 = pl.ds(pl.multiple_of(y0 + HY1, 8), HY - HY1)
     rows_x, rows_z = pl.ds(0, RX), pl.ds(RX, RZ)
+    rows_xz, rows_zx = pl.ds(RS, RX - RS), pl.ds(RX, RZ - RS)
+
+    def strip(first, size, y_):
+        return pl.ds(pl.multiple_of(first + lax.div(y_, 2) * size, 8), size)
+
+    rows_xy, rows_zy, rows_q = strip(0, HS, y), strip(Y0 - RS, HS, y), strip(RS, HXZ, y)
     for d in range(2):
         wait(rx.at[d], rs1.at[d])
     for k in range(4):
         p[x, k, :, rows_x, :] += rx[0, k] + rx[1, k]
     for d in range(1, 4):
-        z_ = mod4(z + d)
-        send(p.at[x, z_, :, rows_x, :], rx2.at[d - 1], ss2.at[d - 1], rs2.at[d - 1], dev(x, y, z_, c))
+        y_, z_ = mod4(y + d), mod4(z + d)
+        send(p.at[x, z_, :, rows_xz, :], rx2.at[d - 1], ss2.at[d - 1], rs2.at[d - 1], dev(x, y, z_, c))
+        send(p.at[x, :, lax.rem(y_, 2), strip(0, HS, y_), :], rxy.at[d - 1], ss2.at[11 + d], rs2.at[11 + d], dev(x, y_, z, c))
     for d in range(2):
         wait(rz.at[d], rs1.at[2 + d])
     for k in range(4):
         p[k, z, :, rows_z, :] += rz[0, k] + rz[1, k]
     for d in range(1, 4):
-        x_ = mod4(x + d)
-        send(p.at[x_, z, :, rows_z, :], rz2.at[d - 1], ss2.at[2 + d], rs2.at[2 + d], dev(x_, y, z, c))
+        x_, y_ = mod4(x + d), mod4(y + d)
+        send(p.at[x_, z, :, rows_zx, :], rz2.at[d - 1], ss2.at[2 + d], rs2.at[2 + d], dev(x_, y, z, c))
+        send(p.at[:, z, lax.rem(y_, 2), strip(Y0 - RS, HS, y_), :], rzy.at[d - 1], ss2.at[14 + d], rs2.at[14 + d], dev(x, y_, z, c))
     slot(1)
     for d in range(2):
         wait(ry.at[d], rs1.at[4 + d])
@@ -380,14 +397,25 @@
 
     for d in range(3):
         wait(rx2.at[d], rs2.at[d])
-    p[x, z, :, rows_x, :] += rx2[0] + rx2[1] + rx2[2]
+    p[x, z, :, rows_xz, :] += rx2[0] + rx2[1] + rx2[2]
     for d in range(3):
         wait(rz2.at[d], rs2.at[3 + d])
-    p[x, z, :, rows_z, :] += rz2[0] + rz2[1] + rz2[2]
+    p[x, z, :, rows_zx, :] += rz2[0] + rz2[1] + rz2[2]
     for d in range(1, 4):
         y_ = mod4(y + d)
-        rows = pl.ds(pl.multiple_of(lax.div(y_, 2) * HXZ, 8), HXZ)
-        send(p.at[x, z, lax.rem(y_, 2), rows, :], rq3.at[d - 1], ss3.at[d - 1], rs3.at[d - 1], dev(x, y_, z, c))
+        send(p.at[x, z, lax.rem(y_, 2), strip(RS, HXZ, y_), :], rq3.at[d - 1], ss3.at[d - 1], rs3.at[d - 1], dev(x, y_, z, c))
+    for d in range(3):
+        wait(rxy.at[d], rs2.at[12 + d])
+    p[x, :, ch, rows_xy, :] += rxy[0] + rxy[1] + rxy[2]
+    for d in range(1, 4):
+        z_ = mod4(z + d)
+        send(p.at[x, z_, ch, rows_xy, :], rxy3.at[d - 1], ss3.at[8 + d], rs3.at[8 + d], dev(x, y, z_, c))
+    for d in range(3):
+        wait(rzy.at[d], rs2.at[15 + d])
+    p[:, z, ch, rows_zy, :] += rzy[0] + rzy[1] + rzy[2]
+    for d in range(1, 4):
+        x_ = mod4(x + d)
+        send(p.at[x_, z, ch, rows_zy, :], rzy3.at[d - 1], ss3.at[11 + d], rs3.at[11 + d], dev(x_, y, z, c))
     for d in range(3):
         wait(ry1.at[d], rs2.at[6 + d])
     p[x, :, ch, rows_1, :] += ry1[0] + ry1[1] + ry1[2]
@@ -403,20 +431,16 @@
 
     slot(3)
 
-    rows_q = pl.ds(pl.multiple_of(lax.div(y, 2) * HXZ, 8), HXZ)
-    for d in range(3):
-        wait(rq3.at[d], rs3.at[d])
-    cb[ch, rows_q, :] = p[x, z, ch, rows_q, :] + (rq3[0] + rq3[1] + rq3[2])
-    for d in range(1, 4):
-        send(cb.at[ch, rows_q, :], cb.at[ch, rows_q, :], ss4.at[d - 1], rs4.at[d - 1], dev(x, mod4(y + d), z, c))
-    for d in range(3):
-        wait(ry13.at[d], rs3.at[3 + d])
-        wait(ry23.at[d], rs3.at[6 + d])
-    cb[ch, rows_1, :] = p[x, z, ch, rows_1, :] + (ry13[0] + ry13[1] + ry13[2])
-    cb[ch, rows_2, :] = p[x, z, ch, rows_2, :] + (ry23[0] + ry23[1] + ry23[2])
-    for d in range(1, 4):
-        send(cb.at[ch, rows_y, :], cb.at[ch, rows_y, :], ss4.at[d + 2], rs4.at[d + 2], dev(x, mod4(y + d), z, c))
-
+    for rows, got, first in (
+        (rows_q, rq3, 0), (rows_xy, rxy3, 9), (rows_zy, rzy3, 12), (rows_1, ry13, 3), (rows_2, ry23, 6),
+    ):
+        for d in range(3):
+            wait(got.at[d], rs3.at[first + d])
+        cb[ch, rows, :] = p[x, z, ch, rows, :] + (got[0] + got[1] + got[2])
+        done = rows_y if got is ry23 else rows
+        if got is not ry13:
+            for d in range(1, 4):
+                send(cb.at[ch, done, :], cb.at[ch, done, :], ss4.at[d - 1], rs4.at[d - 1], dev(x, mod4(y + d), z, c))
     slot(4)
 
     def sent(t, carry):
@@ -439,11 +463,13 @@
         wait(rq3.at[d], ss3.at[d])
         wait(ry13.at[d], ss3.at[3 + d])
         wait(ry23.at[d], ss3.at[6 + d])
-        wait(rq3.at[d], ss4.at[d])
-        wait(cb.at[ch, rows_y, :], ss4.at[3 + d])
-    for d in range(3):
-        wait(rq3.at[d], rs4.at[d])
-        wait(cb.at[ch, rows_y, :], rs4.at[3 + d])
+        wait(rxy.at[d], ss2.at[12 + d])
+        wait(rzy.at[d], ss2.at[15 + d])
+        wait(rxy3.at[d], ss3.at[9 + d])
+        wait(rzy3.at[d], ss3.at[12 + d])
+        wait(cb.at[ch, pl.ds(0, 128), :], ss4.at[d])
+    for d in range(3):
+        wait(cb.at[ch, pl.ds(0, 128), :], rs4.at[d])
     for h in range(2):
         out[:, 128 * h : 128 * h + 128] = mm32(em[...], cb[h])
 
@@ -462,10 +488,11 @@
             vmem((4, 4, 2, 256, 128), F32), vmem((4, 4, 2, 256, 128), F32), vmem((4, 4, 2, 256, 128), F32), vmem((2, 256, 128), F32),
             vmem((2, 4, RX, 128), F32), vmem((2, 4, RZ, 128), F32), vmem((4, 4, HY, 128), F32),
             vmem((2, 4, 2, RX, 128), F32), vmem((2, 4, 2, RZ, 128), F32), vmem((2, 4, 4, HY, 128), F32),
-            vmem((3, 2, RX, 128), F32), vmem((3, 2, RZ, 128), F32), vmem((3, 4, HY1, 128), F32), vmem((3, 4, HY - HY1, 128), F32),
-            vmem((3, HXZ, 128), F32), vmem((3, HY1, 128), F32), vmem((3, HY - HY1, 128), F32), vmem((256, 256), F32),
+            vmem((3, 2, RX - RS, 128), F32), vmem((3, 2, RZ - RS, 128), F32), vmem((3, 4, HY1, 128), F32), vmem((3, 4, HY - HY1, 128), F32),
+            vmem((3, HXZ, 128), F32), vmem((3, HY1, 128), F32), vmem((3, HY - HY1, 128), F32),
+            vmem((3, 4, HS, 128), F32), vmem((3, 4, HS, 128), F32), vmem((3, HS, 128), F32), vmem((3, HS, 128), F32), vmem((256, 256), F32),
             dma((NK,)), dma((NK,)), dma((10,)), dma((16,)), dma((16,)),
-            dma((3,)), dma((8,)), dma((8,)), dma((16,)), dma((3,)), dma((6,)), dma((12,)), dma((12,)), dma((9,)), dma((9,)), dma((6,)), dma((6,)),
+            dma((3,)), dma((8,)), dma((8,)), dma((16,)), dma((3,)), dma((6,)), dma((18,)), dma((18,)), dma((15,)), dma((15,)), dma((3,)), dma((3,)),
         ],
         compiler_params=pltpu.CompilerParams(collective_id=0, has_side_effects=True, vmem_limit_bytes=56 << 20),
         cost_estimate=pl.CostEstimate(flops=9_000_000_000, bytes_accessed=22_000_000, transcendentals=0),

time: 53.3 us -> 52.7 us (0.989)
  Pallas kernels: 51.4 us -> 50.8 us
    pallas_call x1, Pallas kernels: 51.4 us -> 50.8 us  [local(): pl.pallas_call(kernel, out_shape=jax.ShapeDtypeStruct((256, 256), F32), i...]
where the time goes in v5:
time: 52.7 us; the launch traced here: 52.6 us
  Pallas kernels  50.8 us (96%)
  local copies, waits for them, and re-layouts  1.79 us (3%)
    pallas_call x1, Pallas kernels, local(): pl.pallas_call(kernel, out_shape=jax.ShapeDtypeStruct((256, 256), F32), i...  50.8 us
    transpose x1, local copies, waits for them, and re-layouts, local(): return pl.pallas_call(kernel, out_shape=jax.ShapeDtypeStruct((256, 256),...  1.79 us

profile of v5, /device:TPU:0, one launch (start us, length us, event | category | flops | bytes accessed | tf_op | source)
XLA Modules:
  0.0 52.6 jit_solution(12670664790133740699)
XLA Ops:
  0.0 50.8 %shard_map.28 = f32[256,256]{1,0:T(8,128)} custom-call(bf16[1024,8192]{1,0:T(8,128)(2,1)} %a_hbm.1, bf16[8192,256]{1,0:T(8,128)(2,1)} %s_hbm.1), custom_call_target="tpu_custom_call" | custom-call | flops 8999999488 | bytes 22000000 | tf_op jit(solution)/shard_map/pallas_call | solution.py:480
  50.8 1.8 %copy.3 = f32[256,256]{1,0:T(8,128)} copy(f32[256,256]{0,1:T(8,128)} %bitcast.1) | data formatting | bytes 524288 | tf_op jit(solution)/shard_map/transpose | solution.py:499

commit v6 on v5

--- a/solution.py
+++ b/solution.py
@@ -94,7 +94,7 @@
 
 
 def kernel(
-    a_hbm, s_hbm, out,
+    a_hbm, s_hbm, c_out, e_out,
     a, s, acc, ht, g, gh, gr, gy, gf, q, r, p, cb,
     qx, qz, qy, rx, rz, ry, rx2, rz2, ry1, ry2, rq3, ry13, ry23, rxy, rzy, rxy3, rzy3, em,
     asem, ssem, gsem, qsem, rsem, ss0, xs0, zs0, ys0, ss1, rs1, ss2, rs2, ss3, rs3, ss4, rs4,
@@ -442,6 +442,7 @@
             for d in range(1, 4):
                 send(cb.at[ch, done, :], cb.at[ch, done, :], ss4.at[d - 1], rs4.at[d - 1], dev(x, mod4(y + d), z, c))
     slot(4)
+    e_out[...] = em[...].T
 
     def sent(t, carry):
         x_, z_ = lax.div(t, 4), lax.rem(t, 4)
@@ -471,17 +472,17 @@
     for d in range(3):
         wait(cb.at[ch, pl.ds(0, 128), :], rs4.at[d])
     for h in range(2):
-        out[:, 128 * h : 128 * h + 128] = mm32(em[...], cb[h])
+        c_out[128 * h : 128 * h + 128, :] = cb[h].T
 
 
 def local(activations, sketch):
     dma = pltpu.SemaphoreType.DMA
     vmem = pltpu.VMEM
-    return pl.pallas_call(
+    cross, inverse = pl.pallas_call(
         kernel,
-        out_shape=jax.ShapeDtypeStruct((256, 256), F32),
+        out_shape=(jax.ShapeDtypeStruct((256, 256), F32),) * 2,
         in_specs=[pl.BlockSpec(memory_space=pl.ANY)] * 2,
-        out_specs=pl.BlockSpec(memory_space=pltpu.VMEM),
+        out_specs=[pl.BlockSpec(memory_space=pltpu.VMEM)] * 2,
         scratch_shapes=[
             vmem((1024, 8192), BF16), vmem((8192, 256), BF16), vmem((1024, 256), F32), vmem((256, 1024), BF16),
             vmem((256, 256), F32), vmem((128, 256), F32), vmem((15, 8, 256), F32), vmem((4, 8, 256), F32), vmem((256, 256), F32),
@@ -496,7 +497,8 @@
         ],
         compiler_params=pltpu.CompilerParams(collective_id=0, has_side_effects=True, vmem_limit_bytes=56 << 20),
         cost_estimate=pl.CostEstimate(flops=9_000_000_000, bytes_accessed=22_000_000, transcendentals=0),
-    )(activations, sketch).T
+    )(activations, sketch)
+    return jnp.dot(cross, inverse, precision=lax.Precision.HIGHEST, preferred_element_type=F32)
 
 
 def solution(mesh):

time: 52.7 us -> 52.6 us (level)
  matrix products: 0 us -> 2.11 us
  local copies, waits for them, and re-layouts: 1.79 us -> 0 us
    dot_general x0 -> x1, matrix products: none -> 2.11 us  [local(): jnp.dot(cross, inverse, precision=lax.Precision.HIGHEST, preferred_elemen...]
    transpose x1 -> x0, local copies, waits for them, and re-layouts: 1.79 us -> none  [local(): return pl.pallas_call(kernel, out_shape=jax.ShapeDtypeStruct((256, 256),...]
where the time goes in v6:
time: 52.6 us; the launch traced here: 52.4 us
  Pallas kernels  50.3 us (96%)
  matrix products  2.11 us (4%)
    pallas_call x1, Pallas kernels, local(): pl.pallas_call(kernel, out_shape=(jax.ShapeDtypeStruct((256, 256), F32),)...  50.3 us
    dot_general x1, matrix products, local(): jnp.dot(cross, inverse, precision=lax.Precision.HIGHEST, preferred_elemen...  2.11 us

profile of v6, /device:TPU:0, one launch (start us, length us, event | category | flops | bytes accessed | tf_op | source)
XLA Modules:
  0.0 52.4 jit_solution(3385610234241127191)
XLA Ops:
  0.0 50.3 %shard_map.28 = (f32[256,256]{1,0:T(8,128)}, f32[256,256]{1,0:T(8,128)}) custom-call(bf16[1024,8192]{1,0:T(8,128)(2,1)} %a_hbm.1, bf16[8192,256]{1,0:T(8,128)(2,1)} %s_hbm.1), custom_call_target="tpu_custom_call" | custom-call | flops 8999999488 | bytes 22000000 | tf_op jit(solution)/shard_map/pallas_call | solution.py:481
  50.3 2.1 %fusion = f32[256,256]{1,0:T(8,128)} fusion(f32[256,256]{1,0:T(8,128)} %get-tuple-element.7, f32[256,256]{1,0:T(8,128)} %get-tuple-element.8), kind=kOutput, calls=%fused_computation | convolution fusion | flops 201326592 | bytes 786432 | tf_op jit(solution)/shard_map/dot_general | solution.py:501
